TPU v7x, 32 devices: a whole 2x2x4 slice. The times are simulated.
32 devices in a mesh: groups: 2 (over x), row: 16 (over z, y, core).
Axes of the slice: x: 2, y: 2, z: 4, core: 2. Of those that a mesh axis runs over, the one named last changes fastest.
Arguments:
- alignment_features: bfloat16 [512, 512, 256], P(('groups', 'row')), parts along dimension 0, may hold values from -6 to 6
- standardizer_gain: float32 [256], replicated, may hold values from 0.1 to 1.9
- standardizer_shift: float32 [256], replicated, may hold values from -3 to 3
- first_factor_kernel: bfloat16 [256, 32], replicated, may hold values from -0.375 to 0.375
- first_factor_shift: float32 [32], replicated, may hold values from -3 to 3
- second_factor_kernel: bfloat16 [256, 32], replicated, may hold values from -0.375 to 0.375
- second_factor_shift: float32 [32], replicated, may hold values from -3 to 3
- final_map_kernel: bfloat16 [1024, 128], replicated, may hold values from -0.75 to 0.75
- final_map_shift: float32 [128], replicated, may hold values from -3 to 3
Outputs:
- pair_update: bfloat16 [1024, 512, 128], P(('groups', 'row')), parts along dimension 0
There are 2 independent parts, one for each index of `groups`. A program takes and returns all parts, laid end to end along the dimension named above; an argument that names none is the same for every part. Nothing has to cross between parts.
All inputs are finite; a program needn't handle non-finite values.
Results may differ from a plain program's by a relative error of at most 0.0055.
Values may be sent and summed in bfloat16 or wider, within the bound.
A program may use at most 128 MiB of HBM per device.

v0:
```python
import jax
import jax.numpy as jnp
from jax import lax
from jax.sharding import PartitionSpec as P


def largest_divisor(total, limit):
    return max((factor for factor in range(1, min(total, limit) + 1) if total % factor == 0))


def project_flat(
    block,
    standardizer_gain,
    standardizer_shift,
    first_factor_kernel,
    first_factor_shift,
    second_factor_kernel,
    second_factor_shift,
):
    incoming_features = block.astype(jnp.float32)
    center = incoming_features - jnp.mean(incoming_features, axis=-1, keepdims=True)
    spread = jnp.mean(center * center, axis=-1, keepdims=True)
    normed = (center * lax.rsqrt(spread + 1e-05) * standardizer_gain + standardizer_shift).astype(
        jnp.bfloat16
    )
    lines, residues = (normed.shape[0], normed.shape[1])
    first_mapped = jnp.einsum(
        "src,ck->srk", normed, first_factor_kernel, preferred_element_type=jnp.float32
    )
    second_mapped = jnp.einsum(
        "src,ck->srk", normed, second_factor_kernel, preferred_element_type=jnp.float32
    )
    first_flat = (first_mapped + first_factor_shift).astype(jnp.bfloat16).reshape(lines, -1)
    second_flat = (second_mapped + second_factor_shift).astype(jnp.bfloat16).reshape(lines, -1)
    return (first_flat, second_flat)


def pair_rows(left_flat, right_flat, width, final_map_kernel, final_map_shift):
    count = left_flat.shape[0]
    rows = left_flat.shape[1] // width
    cols = right_flat.shape[1] // width
    pair_width = final_map_kernel.shape[1]
    row_step = largest_divisor(rows, max(1, 2048 // cols))
    kernel_grid = final_map_kernel.reshape(width, width, pair_width)

    def one_block(index):
        left_part = lax.dynamic_slice_in_dim(
            left_flat, index * (row_step * width), row_step * width, 1
        )
        outer = lax.dot_general(
            left_part, right_flat, (((0,), (0,)), ((), ())), preferred_element_type=jnp.float32
        )
        outer = (outer / count).astype(jnp.bfloat16).reshape(row_step, width, cols, width)
        mapped = jnp.einsum("icjd,cdp->ijp", outer, kernel_grid, preferred_element_type=jnp.float32)
        return (mapped + final_map_shift).astype(jnp.bfloat16)

    blocks = lax.map(one_block, jnp.arange(rows // row_step, dtype=jnp.int32))
    return blocks.reshape(rows, cols, pair_width)


def body(
    alignment_features,
    standardizer_gain,
    standardizer_shift,
    first_factor_kernel,
    first_factor_shift,
    second_factor_kernel,
    second_factor_shift,
    final_map_kernel,
    final_map_shift,
):
    width = first_factor_kernel.shape[1]
    arrived_lines = lax.all_to_all(
        alignment_features, "row", split_axis=1, concat_axis=0, tiled=True
    )
    left_flat, right_flat = project_flat(
        arrived_lines,
        standardizer_gain,
        standardizer_shift,
        first_factor_kernel,
        first_factor_shift,
        second_factor_kernel,
        second_factor_shift,
    )
    return pair_rows(
        left_flat,
        lax.all_gather(right_flat, "row", axis=1, tiled=True),
        width,
        final_map_kernel,
        final_map_shift,
    )


def solution(mesh):
    return jax.shard_map(
        body,
        mesh=mesh,
        in_specs=(P(("groups", "row"), None, None), P(), P(), P(), P(), P(), P(), P(), P()),
        out_specs=P(("groups", "row"), None, None),
        check_vma=False,
    )
```

profile of v0, /device:TPU:0, one launch (start us, length us, event | category | flops | bytes accessed | tf_op | source)
XLA Modules:
  0.0 506.8 jit_solution(3822944835641388611)
XLA Ops:
  6.5 0.0 copy-start
  6.5 0.0 all-gather.2.cloned.1.call-start
  6.5 4.6 copy.60
  11.1 99.4 %all_to_all.4 = bf16[16,512,256]{2,0,1:T(8,128)(2,1)S(1)} all-to-all(bf16[16,512,256]{2,0,1:T(8,128)(2,1)S(1)} %copy.60), channel_id=1, replica_groups=mesh['groups'=2,'row'=16] {'row'}, dimensions={1} | all-to-all | bytes 8388608 | tf_op jit(solution)/shard_map/all_to_all | solution.py:73
  110.6 1.6 fusion.17
  112.2 1.2 fusion.12
  113.3 2.4 multiply_reduce_fusion
  115.9 0.0 copy-start.4
  115.9 0.0 copy-start.5
  115.9 1.7 copy.62
  117.6 0.0 copy-done.4
  117.6 0.0 copy-done.5
  117.6 3.1 fusion.11
  120.8 0.0 copy-start.2
  120.8 2.0 copy-done.2
  122.7 0.0 copy-done
  122.7 3.2 fusion.13
  126.0 3.5 copy.66
  129.5 0.0 copy-start.7
  129.5 1.0 add_convert_fusion
  130.5 0.0 all-gather.2.cloned.1.call-update
  130.5 0.0 copy-done.3
  130.5 5.3 %fusion.15 = f32[256,32,32]{2,1,0:T(8,128)} fusion(bf16[256,32,256]{2,1,0:T(8,128)(2,1)} %copy-done.2, bf16[256,32]{0,1:T(8,128)(2,1)S(1)} %copy-done.3), kind=kOutput, calls=%fused_computation.24 | convolution fusion | flops 134217728 | bytes 5259264 | tf_op jit(solution)/shard_map/src,ck->srk/dot_general | solution.py:27
  135.9 3.5 copy.65
  139.4 0.2 add_convert_fusion.1
  139.5 0.0 copy-start.8
  139.6 0.0 copy-start.9
  139.6 66.6 %all-gather.2.cloned.1.call-done = bf16[256,16384]{0,1:T(8,128)(2,1)} async-done(((bf16[256,1024]{0,1:T(8,128)(2,1)}), bf16[256,16384]{0,1:T(8,128)(2,1)}) %all-gather.2.cloned.1.call-update) | async-done | bytes 8388624 | tf_op jit(solution)/shard_map/all_gather | solution.py:87
  206.2 12.0 %copy.68 = bf16[256,16384]{1,0:T(8,128)(2,1)} copy(bf16[256,16384]{0,1:T(8,128)(2,1)} %all-gather.2.cloned.1.call-done) | data formatting | bytes 16777216 | tf_op jit(solution)/shard_map/while | solution.py:57
  218.1 0.0 copy-done.9
  218.1 281.1 %while.10 = (s32[]{:T(128)}, bf16[8,4,512,128]{3,2,1,0:T(8,128)(2,1)}, s32[8]{0:T(128)S(1)}, bf16[256,1024]{0,1:T(8,128)(2,1)S(1)}, bf16[256,16384]{1,0:T(8,128)...) while((s32[]{:T(128)}, ...), condition=%wide.region_3.4_spmd, body=%wide.region_2.3_spmd.sunk | while | flops 1615331328 | bytes 38601896 | solution.py:57
  218.4 0.6 dynamic_slice.12
  219.6 6.7 %fusion.32 = bf16[128,16384]{1,0:T(8,128)(2,1)} fusion(bf16[256,16384]{1,0:T(8,128)(2,1)} %get-tuple-element.170, bf16[256,1024]{0,1:T(8,128)(2,1)S(1)} %get-tuple-element.169, s32[]{:T(128)S(6)} %select_n.4), kind=kOutput, calls=%fused_computation.1.clone.1 | convolution fusion | flops 1077936128 | bytes 12648452 | tf_op jit(solution)/shard_map/while/body/eval_jaxpr/dot_general | solution.py:50
  226.3 17.3 %reshape.69 = bf16[4,32,512,32]{3,2,1,0:T(8,128)(2,1)} reshape(bf16[128,16384]{1,0:T(8,128)(2,1)} %fusion.32) | data formatting | bytes 8388608 | tf_op jit(solution)/shard_map/while/body/eval_jaxpr/reshape | solution.py:53
  243.6 9.9 %fusion.33 = bf16[8,4,512,128]{3,2,1,0:T(8,128)(2,1)} fusion(bf16[8,4,512,128]{3,2,1,0:T(8,128)(2,1)} %get-tuple-element.156, s32[]{:T(128)} %get-tuple-element.155, bf16[4,32,512,32]{3,2,1,0:T(8,128)(2,1)} %reshape.69, f32[128]{0:T(128)S(1)} %get-tuple-element.172, bf16[32,32,128]{2,1,0:T(8,128)(2,1)S(1)} %get-tuple-element.171), kind=kOutput, calls=%fused_computation.6.clone.1 | convolution fusion | flops 537395200 | bytes 17564672 | tf_op jit(solution)/shard_map/while/body/eval_jaxpr/icjd,cdp->ijp/dot_general | solution.py:54
  253.5 0.6 dynamic_slice.12
  254.8 6.7 %fusion.32 = bf16[128,16384]{1,0:T(8,128)(2,1)} fusion(bf16[256,16384]{1,0:T(8,128)(2,1)} %get-tuple-element.170, bf16[256,1024]{0,1:T(8,128)(2,1)S(1)} %get-tuple-element.169, s32[]{:T(128)S(6)} %select_n.4), kind=kOutput, calls=%fused_computation.1.clone.1 | convolution fusion | flops 1077936128 | bytes 12648452 | tf_op jit(solution)/shard_map/while/body/eval_jaxpr/dot_general | solution.py:50
  261.4 17.3 %reshape.69 = bf16[4,32,512,32]{3,2,1,0:T(8,128)(2,1)} reshape(bf16[128,16384]{1,0:T(8,128)(2,1)} %fusion.32) | data formatting | bytes 8388608 | tf_op jit(solution)/shard_map/while/body/eval_jaxpr/reshape | solution.py:53
  278.7 9.9 %fusion.33 = bf16[8,4,512,128]{3,2,1,0:T(8,128)(2,1)} fusion(bf16[8,4,512,128]{3,2,1,0:T(8,128)(2,1)} %get-tuple-element.156, s32[]{:T(128)} %get-tuple-element.155, bf16[4,32,512,32]{3,2,1,0:T(8,128)(2,1)} %reshape.69, f32[128]{0:T(128)S(1)} %get-tuple-element.172, bf16[32,32,128]{2,1,0:T(8,128)(2,1)S(1)} %get-tuple-element.171), kind=kOutput, calls=%fused_computation.6.clone.1 | convolution fusion | flops 537395200 | bytes 17564672 | tf_op jit(solution)/shard_map/while/body/eval_jaxpr/icjd,cdp->ijp/dot_general | solution.py:54
  288.6 0.6 dynamic_slice.12
  289.9 6.7 %fusion.32 = bf16[128,16384]{1,0:T(8,128)(2,1)} fusion(bf16[256,16384]{1,0:T(8,128)(2,1)} %get-tuple-element.170, bf16[256,1024]{0,1:T(8,128)(2,1)S(1)} %get-tuple-element.169, s32[]{:T(128)S(6)} %select_n.4), kind=kOutput, calls=%fused_computation.1.clone.1 | convolution fusion | flops 1077936128 | bytes 12648452 | tf_op jit(solution)/shard_map/while/body/eval_jaxpr/dot_general | solution.py:50
  296.5 17.3 %reshape.69 = bf16[4,32,512,32]{3,2,1,0:T(8,128)(2,1)} reshape(bf16[128,16384]{1,0:T(8,128)(2,1)} %fusion.32) | data formatting | bytes 8388608 | tf_op jit(solution)/shard_map/while/body/eval_jaxpr/reshape | solution.py:53
  313.8 9.9 %fusion.33 = bf16[8,4,512,128]{3,2,1,0:T(8,128)(2,1)} fusion(bf16[8,4,512,128]{3,2,1,0:T(8,128)(2,1)} %get-tuple-element.156, s32[]{:T(128)} %get-tuple-element.155, bf16[4,32,512,32]{3,2,1,0:T(8,128)(2,1)} %reshape.69, f32[128]{0:T(128)S(1)} %get-tuple-element.172, bf16[32,32,128]{2,1,0:T(8,128)(2,1)S(1)} %get-tuple-element.171), kind=kOutput, calls=%fused_computation.6.clone.1 | convolution fusion | flops 537395200 | bytes 17564672 | tf_op jit(solution)/shard_map/while/body/eval_jaxpr/icjd,cdp->ijp/dot_general | solution.py:54
  323.7 0.6 dynamic_slice.12
  325.0 6.7 %fusion.32 = bf16[128,16384]{1,0:T(8,128)(2,1)} fusion(bf16[256,16384]{1,0:T(8,128)(2,1)} %get-tuple-element.170, bf16[256,1024]{0,1:T(8,128)(2,1)S(1)} %get-tuple-element.169, s32[]{:T(128)S(6)} %select_n.4), kind=kOutput, calls=%fused_computation.1.clone.1 | convolution fusion | flops 1077936128 | bytes 12648452 | tf_op jit(solution)/shard_map/while/body/eval_jaxpr/dot_general | solution.py:50
  331.6 17.3 %reshape.69 = bf16[4,32,512,32]{3,2,1,0:T(8,128)(2,1)} reshape(bf16[128,16384]{1,0:T(8,128)(2,1)} %fusion.32) | data formatting | bytes 8388608 | tf_op jit(solution)/shard_map/while/body/eval_jaxpr/reshape | solution.py:53
  348.9 9.9 %fusion.33 = bf16[8,4,512,128]{3,2,1,0:T(8,128)(2,1)} fusion(bf16[8,4,512,128]{3,2,1,0:T(8,128)(2,1)} %get-tuple-element.156, s32[]{:T(128)} %get-tuple-element.155, bf16[4,32,512,32]{3,2,1,0:T(8,128)(2,1)} %reshape.69, f32[128]{0:T(128)S(1)} %get-tuple-element.172, bf16[32,32,128]{2,1,0:T(8,128)(2,1)S(1)} %get-tuple-element.171), kind=kOutput, calls=%fused_computation.6.clone.1 | convolution fusion | flops 537395200 | bytes 17564672 | tf_op jit(solution)/shard_map/while/body/eval_jaxpr/icjd,cdp->ijp/dot_general | solution.py:54
  358.8 0.6 dynamic_slice.12
  360.1 6.7 %fusion.32 = bf16[128,16384]{1,0:T(8,128)(2,1)} fusion(bf16[256,16384]{1,0:T(8,128)(2,1)} %get-tuple-element.170, bf16[256,1024]{0,1:T(8,128)(2,1)S(1)} %get-tuple-element.169, s32[]{:T(128)S(6)} %select_n.4), kind=kOutput, calls=%fused_computation.1.clone.1 | convolution fusion | flops 1077936128 | bytes 12648452 | tf_op jit(solution)/shard_map/while/body/eval_jaxpr/dot_general | solution.py:50
  366.7 17.3 %reshape.69 = bf16[4,32,512,32]{3,2,1,0:T(8,128)(2,1)} reshape(bf16[128,16384]{1,0:T(8,128)(2,1)} %fusion.32) | data formatting | bytes 8388608 | tf_op jit(solution)/shard_map/while/body/eval_jaxpr/reshape | solution.py:53
  384.0 9.9 %fusion.33 = bf16[8,4,512,128]{3,2,1,0:T(8,128)(2,1)} fusion(bf16[8,4,512,128]{3,2,1,0:T(8,128)(2,1)} %get-tuple-element.156, s32[]{:T(128)} %get-tuple-element.155, bf16[4,32,512,32]{3,2,1,0:T(8,128)(2,1)} %reshape.69, f32[128]{0:T(128)S(1)} %get-tuple-element.172, bf16[32,32,128]{2,1,0:T(8,128)(2,1)S(1)} %get-tuple-element.171), kind=kOutput, calls=%fused_computation.6.clone.1 | convolution fusion | flops 537395200 | bytes 17564672 | tf_op jit(solution)/shard_map/while/body/eval_jaxpr/icjd,cdp->ijp/dot_general | solution.py:54
  393.9 0.6 dynamic_slice.12
  395.2 6.7 %fusion.32 = bf16[128,16384]{1,0:T(8,128)(2,1)} fusion(bf16[256,16384]{1,0:T(8,128)(2,1)} %get-tuple-element.170, bf16[256,1024]{0,1:T(8,128)(2,1)S(1)} %get-tuple-element.169, s32[]{:T(128)S(6)} %select_n.4), kind=kOutput, calls=%fused_computation.1.clone.1 | convolution fusion | flops 1077936128 | bytes 12648452 | tf_op jit(solution)/shard_map/while/body/eval_jaxpr/dot_general | solution.py:50
  401.9 17.3 %reshape.69 = bf16[4,32,512,32]{3,2,1,0:T(8,128)(2,1)} reshape(bf16[128,16384]{1,0:T(8,128)(2,1)} %fusion.32) | data formatting | bytes 8388608 | tf_op jit(solution)/shard_map/while/body/eval_jaxpr/reshape | solution.py:53
  419.1 9.9 %fusion.33 = bf16[8,4,512,128]{3,2,1,0:T(8,128)(2,1)} fusion(bf16[8,4,512,128]{3,2,1,0:T(8,128)(2,1)} %get-tuple-element.156, s32[]{:T(128)} %get-tuple-element.155, bf16[4,32,512,32]{3,2,1,0:T(8,128)(2,1)} %reshape.69, f32[128]{0:T(128)S(1)} %get-tuple-element.172, bf16[32,32,128]{2,1,0:T(8,128)(2,1)S(1)} %get-tuple-element.171), kind=kOutput, calls=%fused_computation.6.clone.1 | convolution fusion | flops 537395200 | bytes 17564672 | tf_op jit(solution)/shard_map/while/body/eval_jaxpr/icjd,cdp->ijp/dot_general | solution.py:54
  429.0 0.6 dynamic_slice.12
  430.3 6.7 %fusion.32 = bf16[128,16384]{1,0:T(8,128)(2,1)} fusion(bf16[256,16384]{1,0:T(8,128)(2,1)} %get-tuple-element.170, bf16[256,1024]{0,1:T(8,128)(2,1)S(1)} %get-tuple-element.169, s32[]{:T(128)S(6)} %select_n.4), kind=kOutput, calls=%fused_computation.1.clone.1 | convolution fusion | flops 1077936128 | bytes 12648452 | tf_op jit(solution)/shard_map/while/body/eval_jaxpr/dot_general | solution.py:50
  437.0 17.3 %reshape.69 = bf16[4,32,512,32]{3,2,1,0:T(8,128)(2,1)} reshape(bf16[128,16384]{1,0:T(8,128)(2,1)} %fusion.32) | data formatting | bytes 8388608 | tf_op jit(solution)/shard_map/while/body/eval_jaxpr/reshape | solution.py:53
  454.2 9.9 %fusion.33 = bf16[8,4,512,128]{3,2,1,0:T(8,128)(2,1)} fusion(bf16[8,4,512,128]{3,2,1,0:T(8,128)(2,1)} %get-tuple-element.156, s32[]{:T(128)} %get-tuple-element.155, bf16[4,32,512,32]{3,2,1,0:T(8,128)(2,1)} %reshape.69, f32[128]{0:T(128)S(1)} %get-tuple-element.172, bf16[32,32,128]{2,1,0:T(8,128)(2,1)S(1)} %get-tuple-element.171), kind=kOutput, calls=%fused_computation.6.clone.1 | convolution fusion | flops 537395200 | bytes 17564672 | tf_op jit(solution)/shard_map/while/body/eval_jaxpr/icjd,cdp->ijp/dot_general | solution.py:54
  464.2 0.6 dynamic_slice.12
  465.4 6.7 %fusion.32 = bf16[128,16384]{1,0:T(8,128)(2,1)} fusion(bf16[256,16384]{1,0:T(8,128)(2,1)} %get-tuple-element.170, bf16[256,1024]{0,1:T(8,128)(2,1)S(1)} %get-tuple-element.169, s32[]{:T(128)S(6)} %select_n.4), kind=kOutput, calls=%fused_computation.1.clone.1 | convolution fusion | flops 1077936128 | bytes 12648452 | tf_op jit(solution)/shard_map/while/body/eval_jaxpr/dot_general | solution.py:50
  472.1 17.3 %reshape.69 = bf16[4,32,512,32]{3,2,1,0:T(8,128)(2,1)} reshape(bf16[128,16384]{1,0:T(8,128)(2,1)} %fusion.32) | data formatting | bytes 8388608 | tf_op jit(solution)/shard_map/while/body/eval_jaxpr/reshape | solution.py:53
  489.3 9.9 %fusion.33 = bf16[8,4,512,128]{3,2,1,0:T(8,128)(2,1)} fusion(bf16[8,4,512,128]{3,2,1,0:T(8,128)(2,1)} %get-tuple-element.156, s32[]{:T(128)} %get-tuple-element.155, bf16[4,32,512,32]{3,2,1,0:T(8,128)(2,1)} %reshape.69, f32[128]{0:T(128)S(1)} %get-tuple-element.172, bf16[32,32,128]{2,1,0:T(8,128)(2,1)S(1)} %get-tuple-element.171), kind=kOutput, calls=%fused_computation.6.clone.1 | convolution fusion | flops 537395200 | bytes 17564672 | tf_op jit(solution)/shard_map/while/body/eval_jaxpr/icjd,cdp->ijp/dot_general | solution.py:54
  499.3 0.7 copy-done.1
  (12 shorter events, 0.1 us)
Async XLA Ops:
  6.5 116.2 %copy-start = (bf16[256,32]{0,1:T(8,128)(2,1)S(1)}, bf16[256,32]{0,1:T(8,128)(2,1)}, u32[]{:S(2)}) copy-start(bf16[256,32]{0,1:T(8,128)(2,1)} %param.16) | copy-start | bytes 49156
  6.5 199.6 %all-gather.2.cloned.1.call-start = ((), (), s32[]{:S(2)}) async-start(), calls=%async_computation.1 | async-start | bytes 8912896 | tf_op jit(solution)/shard_map/all_gather | solution.py:87
  115.9 1.7 copy-start.4
  115.9 1.7 copy-start.5
  120.8 2.0 copy-start.2
  122.7 6.8 %copy-start.6 = (f32[32]{0:T(128)S(1)}, f32[32]{0:T(128)}, u32[]{:S(2)}) copy-start(f32[32]{0:T(128)} %param.17) | copy-start | bytes 388
  122.7 7.8 %copy-start.3 = (bf16[256,32]{0,1:T(8,128)(2,1)S(1)}, bf16[256,32]{0,1:T(8,128)(2,1)}, u32[]{:S(2)}) copy-start(bf16[256,32]{0,1:T(8,128)(2,1)} %param.14) | copy-start | bytes 49156
  129.5 9.9 %copy-start.7 = (f32[32]{0:T(128)S(1)}, f32[32]{0:T(128)}, u32[]{:S(2)}) copy-start(f32[32]{0:T(128)} %param.15) | copy-start | bytes 388
  139.5 78.6 %copy-start.8 = (bf16[1024,128]{1,0:T(8,128)(2,1)S(1)}, bf16[1024,128]{1,0:T(8,128)(2,1)}, u32[]{:S(2)}) copy-start(bf16[1024,128]{1,0:T(8,128)(2,1)} %param.18) | copy-start | bytes 786436
  139.6 78.6 %copy-start.9 = (f32[128]{0:T(128)S(1)}, f32[128]{0:T(128)}, u32[]{:S(2)}) copy-start(f32[128]{0:T(128)} %param.19) | copy-start | bytes 1540
  499.3 0.7 copy-start.1
Sparse Core Ops, SparseCore 0:
  130.6 75.4 all-gather.1
where the time goes:
time: 511 us; the launch traced here: 507 us
  local copies, waits for them, and re-layouts  171 us (33%)
  matrix products  141 us (28%)
  blocking collectives  99.4 us (19%)
  waiting for transfers between devices  66.6 us (13%)
  between operations  13.6 us (3%)
  other arithmetic  9.49 us (2%)
  loops' own time  5.28 us (1%)
    reshape x8, local copies, waits for them, and re-layouts, one_block(): (outer / count).astype(jnp.bfloat16).reshape(row_step, width, cols, width)  138 us
    all_to_all x1, blocking collectives, body(): lax.all_to_all(alignment_features, 'row', split_axis=1, concat_axis=0, ti...  99.4 us
    dot_general x8, matrix products, one_block(): jnp.einsum('icjd,cdp->ijp', outer, kernel_grid, preferred_element_type=jn...  79.4 us
    all_gather x1, waiting for transfers between devices, body(): lax.all_gather(right_flat, 'row', axis=1, tiled=True)  66.6 us
    dot_general x8, matrix products, one_block(): lax.dot_general(left_part, right_flat, (((0,), (0,)), ((), ())), preferre...  53.3 us
    while x1, local copies, waits for them, and re-layouts, pair_rows(): blocks = lax.map(one_block, jnp.arange(rows // row_step, dtype=jnp.int32))  12 us
  transfers between devices with their start and end apart: 1, of which 1 were waited for; matrix products, arithmetic and copies ran while one was open for 2% of the time, Pallas kernels for 0%

commit v1 on v0

--- a/solution.py
+++ b/solution.py
@@ -1,7 +1,14 @@
+import functools
+
 import jax
 import jax.numpy as jnp
 from jax import lax
+from jax.experimental import pallas as pl
+from jax.experimental.pallas import tpu as pltpu
 from jax.sharding import PartitionSpec as P
+
+LANES = 128
+SUBLANES = 8
 
 
 def largest_divisor(total, limit):
@@ -56,6 +63,144 @@
 
     blocks = lax.map(one_block, jnp.arange(rows // row_step, dtype=jnp.int32))
     return blocks.reshape(rows, cols, pair_width)
+
+
+def project_kernel(
+    features,
+    gain,
+    offset,
+    first_spread,
+    first_bias,
+    second_t,
+    second_bias,
+    left_out,
+    right_out,
+    first_rows,
+    second_rows,
+):
+    lines, span, depth = features.shape
+    width = second_t.shape[0]
+    fold = LANES // width
+    owners = span // (fold * SUBLANES)
+    incoming = features[...].astype(jnp.float32).reshape(lines * span, depth)
+    center = incoming - jnp.mean(incoming, axis=-1, keepdims=True)
+    spread = jnp.mean(center * center, axis=-1, keepdims=True)
+    normed = center * lax.rsqrt(spread + 1e-05) * gain[...] + offset[...]
+    split = normed.reshape(lines * owners, fold, SUBLANES, depth)
+    folded = jnp.concatenate(
+        [split[:, m].reshape(lines * owners * SUBLANES, depth).astype(jnp.bfloat16) for m in range(fold)],
+        axis=1,
+    )
+    first_rows[...] = (
+        jnp.dot(folded, first_spread[...], preferred_element_type=jnp.float32) + first_bias[...]
+    )
+    flat = normed.astype(jnp.bfloat16)
+    for s in range(lines):
+        second_rows[s * width : (s + 1) * width, :] = (
+            lax.dot_general(
+                second_t[...],
+                flat[s * span : (s + 1) * span],
+                (((1,), (1,)), ((), ())),
+                preferred_element_type=jnp.float32,
+            )
+            + second_bias[...]
+        )
+    per_line = owners * SUBLANES
+    for q in range(per_line):
+        left_out[:, q * LANES : (q + 1) * LANES] = first_rows[
+            pl.ds(q, lines, stride=per_line), :
+        ].astype(jnp.bfloat16)
+    for d in range(width):
+        right_out[:, d * span : (d + 1) * span] = second_rows[
+            pl.ds(d, lines, stride=width), :
+        ].astype(jnp.bfloat16)
+
+
+def project(features, gain, offset, first_kernel, first_bias, second_kernel, second_bias):
+    lines, residues, depth = features.shape
+    width = first_kernel.shape[1]
+    fold = LANES // width
+    chunks = residues // LANES
+    first_spread = jnp.einsum("mn,ck->mcnk", jnp.eye(fold, dtype=first_kernel.dtype), first_kernel)
+    first_spread = first_spread.reshape(fold * depth, LANES)
+    whole = pl.BlockSpec(memory_space=pltpu.VMEM)
+    return pl.pallas_call(
+        project_kernel,
+        grid=(chunks,),
+        in_specs=[pl.BlockSpec((lines, LANES, depth), lambda k: (0, k, 0))] + [whole] * 6,
+        out_specs=[
+            pl.BlockSpec((lines, LANES * width), lambda k: (0, k)),
+            pl.BlockSpec((lines, LANES * width), lambda k: (0, k)),
+        ],
+        out_shape=[jax.ShapeDtypeStruct((lines, residues * width), jnp.bfloat16)] * 2,
+        scratch_shapes=[
+            pltpu.VMEM((lines * LANES // fold, LANES), jnp.float32),
+            pltpu.VMEM((lines * width, LANES), jnp.float32),
+        ],
+        compiler_params=pltpu.CompilerParams(vmem_limit_bytes=48 * 1024 * 1024),
+    )(
+        features,
+        gain.reshape(1, depth),
+        offset.reshape(1, depth),
+        first_spread,
+        jnp.tile(first_bias, fold).reshape(1, LANES),
+        second_kernel.T,
+        second_bias.reshape(width, 1),
+    )
+
+
+def pair_kernel(left_t, right, map_t, map_bias, out, outer):
+    rows, span, pair_width = out.shape
+    count = right.shape[0]
+    width = right.shape[1] // span
+    fold = LANES // width
+
+    @pl.loop(0, width // 2)
+    def _(step):
+        part = jnp.dot(
+            left_t[...],
+            right[:, pl.ds(pl.multiple_of(step * (2 * span), 2 * span), 2 * span)],
+            preferred_element_type=jnp.float32,
+        )
+        part = part.astype(jnp.bfloat16).reshape(rows // 2, 2, width, 2 * span)
+        for half in range(2):
+            place = pl.ds(pl.multiple_of(step * (2 * width) + half * width, width), width)
+            for side in range(2):
+                outer[:, place, side * span : (side + 1) * span] = part[
+                    :, side, :, half * span : (half + 1) * span
+                ]
+
+    @pl.loop(0, rows // 2)
+    def _(pair):
+        mapped = jnp.dot(map_t[...], outer[pair], preferred_element_type=jnp.float32)
+        mapped = mapped * (1.0 / count) + map_bias[...]
+        for side in range(2):
+            block = 2 * pair + side
+            row = (block % fold) * SUBLANES + block // fold
+            out[row] = mapped[:, side * span : (side + 1) * span].T.astype(jnp.bfloat16)
+
+
+def pair_update(left_t, right, final_map_kernel, final_map_bias, rows):
+    count = right.shape[0]
+    pair_width = final_map_kernel.shape[1]
+    width = left_t.shape[0] // rows
+    cols = right.shape[1] // width
+    map_t = final_map_kernel.reshape(width, width, pair_width).transpose(2, 1, 0)
+    whole = pl.BlockSpec(memory_space=pltpu.VMEM)
+    return pl.pallas_call(
+        pair_kernel,
+        grid=(cols // LANES,),
+        in_specs=[
+            whole,
+            pl.BlockSpec((count, LANES * width), lambda k: (0, k)),
+            whole,
+            whole,
+        ],
+        out_specs=pl.BlockSpec((rows, LANES, pair_width), lambda k: (0, k, 0)),
+        out_shape=jax.ShapeDtypeStruct((rows, cols, pair_width), jnp.bfloat16),
+        scratch_shapes=[pltpu.VMEM((rows // 2, width * width, 2 * LANES), jnp.bfloat16)],
+        compiler_params=pltpu.CompilerParams(vmem_limit_bytes=48 * 1024 * 1024),
+    )(left_t, right, map_t.reshape(pair_width, width * width), final_map_bias.reshape(pair_width, 1))
 
 
 def body(
@@ -69,6 +214,37 @@
     final_map_kernel,
     final_map_shift,
 ):
+    left, right = project(
+        alignment_features,
+        standardizer_gain,
+        standardizer_shift,
+        first_factor_kernel,
+        first_factor_shift,
+        second_factor_kernel,
+        second_factor_shift,
+    )
+    rows = alignment_features.shape[1] // lax.axis_size("row")
+    left_t = lax.all_to_all(left, "row", split_axis=1, concat_axis=0, tiled=True).T
+    return pair_update(
+        left_t,
+        lax.all_gather(right, "row", axis=0, tiled=True),
+        final_map_kernel,
+        final_map_shift,
+        rows,
+    )
+
+
+def plain_body(
+    alignment_features,
+    standardizer_gain,
+    standardizer_shift,
+    first_factor_kernel,
+    first_factor_shift,
+    second_factor_kernel,
+    second_factor_shift,
+    final_map_kernel,
+    final_map_shift,
+):
     width = first_factor_kernel.shape[1]
     arrived_lines = lax.all_to_all(
         alignment_features, "row", split_axis=1, concat_axis=0, tiled=True
@@ -92,10 +268,29 @@
 
 
 def solution(mesh):
-    return jax.shard_map(
-        body,
-        mesh=mesh,
-        in_specs=(P(("groups", "row"), None, None), P(), P(), P(), P(), P(), P(), P(), P()),
-        out_specs=P(("groups", "row"), None, None),
-        check_vma=False,
-    )
+    ways = mesh.shape["row"]
+    groups = mesh.shape["groups"]
+
+    def update(alignment_features, *parameters):
+        total, residues, depth = alignment_features.shape
+        width = parameters[2].shape[1]
+        lines = total // (groups * ways)
+        count = lines * ways
+        fits = (
+            ways == 16
+            and lines % 16 == 0
+            and count & (count - 1) == 0
+            and width == 32
+            and residues == 32 * ways
+            and depth % LANES == 0
+            and parameters[6].shape[1] == LANES
+        )
+        return jax.shard_map(
+            body if fits else plain_body,
+            mesh=mesh,
+            in_specs=(P(("groups", "row"), None, None),) + (P(),) * len(parameters),
+            out_specs=P(("groups", "row"), None, None),
+            check_vma=False,
+        )(alignment_features, *parameters)
+
+    return update

time: 511 us -> 158 us (0.31)
  local copies, waits for them, and re-layouts: 171 us -> 7.38 us
  matrix products: 141 us -> 0 us
  blocking collectives: 99.4 us -> 0 us
  Pallas kernels: 0 us -> 51.3 us
  waiting for transfers between devices: 66.6 us -> 77.2 us
  other arithmetic: 9.49 us -> 0.9 us
  starting transfers between devices: 0.01 us -> 7.39 us
  loops' own time: 5.28 us -> 0 us
    dot_general x18 -> x0, matrix products: 141 us -> none  [the longest x8 79.4 us: one_block(): jnp.einsum('icjd,cdp->ijp', outer, kernel_grid, preferred_element_type=jn...]
    reshape x8 -> x4, local copies, waits for them, and re-layouts: 138 us -> 1.16 us  [the longest x1 0.74 us: project(): second_bias.reshape(width, 1)]
    all_to_all x1 -> x0, blocking collectives: 99.4 us -> none  [body(): lax.all_to_all(alignment_features, 'row', split_axis=1, concat_axis=0, ti...]
    pallas_call x0 -> x2, Pallas kernels: none -> 51.3 us  [the longest x1 44.6 us: pair_update(): pl.pallas_call(pair_kernel, grid=(cols // LANES,), in_specs=[whole, pl.Bl...]
    all_to_all x0 -> x1, waiting for transfers between devices: none -> 20.2 us  [body(): lax.all_to_all(left, 'row', split_axis=1, concat_axis=0, tiled=True)]
    while x1 -> x0, local copies, waits for them, and re-layouts: 12 us -> none  [pair_rows(): blocks = lax.map(one_block, jnp.arange(rows // row_step, dtype=jnp.int32))]
    all_gather x1, waiting for transfers between devices: 66.6 us -> 57 us  [body(): lax.all_gather(right, 'row', axis=0, tiled=True)]
    all_to_all x0 -> x1, starting transfers between devices: none -> 7.38 us  [body(): lax.all_to_all(left, 'row', split_axis=1, concat_axis=0, tiled=True)]
  transfers between devices with their start and end apart: 1 -> 2, of which waited for: 1 -> 2; matrix products, arithmetic and copies ran while one was open for 2% -> 1% of each run, Pallas kernels for 0% -> 0%
where the time goes in v1:
time: 158 us
  waiting for transfers between devices  77.2 us (49%)
  Pallas kernels  51.3 us (32%)
  between operations  13.5 us (9%)
  starting transfers between devices  7.39 us (5%)
  local copies, waits for them, and re-layouts  7.38 us (5%)
    all_gather x1, waiting for transfers between devices, body(): lax.all_gather(right, 'row', axis=0, tiled=True)  57 us
    pallas_call x1, Pallas kernels, pair_update(): pl.pallas_call(pair_kernel, grid=(cols // LANES,), in_specs=[whole, pl.Bl...  44.6 us
    all_to_all x1, waiting for transfers between devices, body(): lax.all_to_all(left, 'row', split_axis=1, concat_axis=0, tiled=True)  20.2 us
    all_to_all x1, starting transfers between devices, body(): lax.all_to_all(left, 'row', split_axis=1, concat_axis=0, tiled=True)  7.38 us
    pallas_call x1, Pallas kernels, project(): pl.pallas_call(project_kernel, grid=(chunks,), in_specs=[pl.BlockSpec((li...  6.79 us
    unnamed x13, local copies, waits for them, and re-layouts  4.3 us
  transfers between devices with their start and end apart: 2, of which 2 were waited for; matrix products, arithmetic and copies ran while one was open for 1% of the time, Pallas kernels for 0%

profile of v1, /device:TPU:0, one launch (start us, length us, event | category | flops | bytes accessed | tf_op | source)
XLA Modules:
  0.0 157.7 jit_solution(16384184173034165057)
XLA Ops:
  6.5 0.0 all-gather.2.cloned.1.call-start
  6.5 0.7 tile.2
  7.2 0.1 reshape_tile.3.first_bias
  7.3 0.7 copy.22.second_bias
  8.0 0.0 copy-start.5
  8.0 0.9 broadcast_multiply_fusion
  8.9 0.0 copy-start.4
  9.0 0.2 copy.21.first_spread
  9.1 0.0 copy-start
  9.2 2.2 %copy-done = bf16[16,512,256]{2,1,0:T(8,128)(2,1)S(1)} copy-done((bf16[16,512,256]{2,1,0:T(8,128)(2,1)S(1)}, bf16[16,512,256]{2,1,0:T(8,128)(2,1)}, u32[]{:S(2)}) %copy-start) | copy-done | bytes 4194328
  11.3 0.0 copy-start.1
  11.3 0.7 copy-done.1
  12.1 0.0 copy-start.2
  12.1 0.7 copy-done.2
  12.7 0.0 copy-start.3
  12.7 0.7 copy-done.3
  13.4 6.8 %shard_map.91 = (bf16[16,16384]{1,0:T(8,128)(2,1)S(1)}, bf16[16,16384]{1,0:T(8,128)(2,1)}) custom-call(bf16[16,512,256]{2,1,0:T(8,128)(2,1)S(1)} %copy-done, f32[1,256]{1,0:T(1,128)S(1)} %bitcast.26, f32[1,256]{1,0:T(1,128)S(1)} %bitcast.27, bf16[1024,128]{1,0:T(8,128)(2,1)S(1)} %copy.21.first_spread, f32[1,128]{1,0:T(1,128)S(1)} %reshape_tile.3.first_bias, ...), custom_call_target="tpu_custom_call" | custom-call | tf_op jit(solution)/shard_map/pallas_call | solution.py:127
  20.2 0.0 all-gather.2.cloned.1.call-update
  20.2 0.9 copy.31
  21.1 7.4 %all-to-all-start = ((bf16[16,16,1024]{2,0,1:T(8,128)(2,1)}), bf16[16,16,1024]{2,0,1:T(8,128)(2,1)S(1)}, u32[]{:S(2)}, u32[]{:S(2)}) async-start(bf16[16,16,1024]{2,0,1:T(8,128)(2,1)} %bitcast.22), calls=%async_computation | async-start | bytes 1048576 | tf_op jit(solution)/shard_map/all_to_all | solution.py:227
  28.5 0.0 copy-done.5
  28.5 0.1 copy.27.map_bias
  28.6 0.0 copy-done.4
  28.6 0.1 copy.25
  28.7 0.1 copy.26.map_t
  28.9 20.2 %all-to-all-done = bf16[16,16,1024]{2,0,1:T(8,128)(2,1)S(1)} async-done(((bf16[16,16,1024]{2,0,1:T(8,128)(2,1)}), bf16[16,16,1024]{2,0,1:T(8,128)(2,1)S(1)}, u32[]{:S(2)}, u32[]{:S(2)}) %all-to-all-start) | async-done | bytes 524320 | tf_op jit(solution)/shard_map/all_to_all | solution.py:227
  49.1 0.2 copy.24
  49.3 57.0 %all-gather.2.cloned.1.call-done.right = bf16[256,16384]{1,0:T(8,128)(2,1)} async-done(((bf16[16,16384]{1,0:T(8,128)(2,1)}), bf16[256,16384]{1,0:T(8,128)(2,1)}) %all-gather.2.cloned.1.call-update) | async-done | bytes 8388624 | tf_op jit(solution)/shard_map/all_gather | solution.py:230
  106.3 44.6 %shard_map.92 = bf16[32,512,128]{2,1,0:T(8,128)(2,1)} custom-call(bf16[1024,256]{1,0:T(8,128)(2,1)S(1)} %bitcast.23, bf16[256,16384]{1,0:T(8,128)(2,1)} %all-gather.2.cloned.1.call-done.right, bf16[128,1024]{1,0:T(8,128)(2,1)S(1)} %copy.26.map_t, f32[128,1]{1,0:T(8,128)S(1)} %copy.27.map_bias), custom_call_target="tpu_custom_call" | custom-call | tf_op jit(solution)/shard_map/pallas_call | solution.py:190
  (2 shorter events, 0.0 us)
Async XLA Ops:
  6.5 99.7 %all-gather.2.cloned.1.call-start = ((), (), s32[]{:S(2)}) async-start(), calls=%async_computation.1 | async-start | bytes 8912896 | tf_op jit(solution)/shard_map/all_gather | solution.py:230
  8.0 20.5 %copy-start.5 = (f32[128]{0:T(128)S(1)}, f32[128]{0:T(128)}, u32[]{:S(2)}) copy-start(f32[128]{0:T(128)} %param.17) | copy-start | bytes 1540
  8.9 19.7 %copy-start.4 = (bf16[1024,128]{1,0:T(8,128)(2,1)S(1)}, bf16[1024,128]{1,0:T(8,128)(2,1)}, u32[]{:S(2)}) copy-start(bf16[1024,128]{1,0:T(8,128)(2,1)} %param.16) | copy-start | bytes 786436
  9.1 2.2 %copy-start = (bf16[16,512,256]{2,1,0:T(8,128)(2,1)S(1)}, bf16[16,512,256]{2,1,0:T(8,128)(2,1)}, u32[]{:S(2)}) copy-start(bf16[16,512,256]{2,1,0:T(8,128)(2,1)} %features.1) | copy-start | bytes 12582916
  11.3 0.7 copy-start.1
  12.1 0.7 copy-start.2
  12.7 0.7 copy-start.3
  21.1 28.0 %all-to-all-start = ((bf16[16,16,1024]{2,0,1:T(8,128)(2,1)}), bf16[16,16,1024]{2,0,1:T(8,128)(2,1)S(1)}, u32[]{:S(2)}, u32[]{:S(2)}) async-start(bf16[16,16,1024]{2,0,1:T(8,128)(2,1)} %bitcast.22), calls=%async_computation | async-start | bytes 1048576 | tf_op jit(solution)/shard_map/all_to_all | solution.py:227
Sparse Core Ops, SparseCore 0:
  20.4 85.8 all-gather.1

commit v2 on v1

--- a/solution.py
+++ b/solution.py
@@ -149,58 +149,267 @@
     )
 
 
-def pair_kernel(left_t, right, map_t, map_bias, out, outer):
-    rows, span, pair_width = out.shape
-    count = right.shape[0]
-    width = right.shape[1] // span
+MESH = pl.DeviceIdType.MESH
+
+
+def fused_kernel(
+    ways,
+    left_in,
+    right_in,
+    map_t,
+    map_bias,
+    out,
+    held,
+    left_held,
+    left_t,
+    outer,
+    left_send,
+    left_recv,
+    ring_send,
+    ring_recv,
+    share_send,
+    share_recv,
+):
+    chunks, count, chunk_lanes = held.shape
+    lines = right_in.shape[0]
+    left_lanes = left_held.shape[1]
+    rows = out.shape[0]
+    span = LANES
+    width = chunk_lanes // span
     fold = LANES // width
-
-    @pl.loop(0, width // 2)
+    chips = ways // 2
+    side_chips = chips // 2
+    half_lanes = chunk_lanes // 2
+    far = chips // 2
+
+    me = lax.axis_index("row")
+    core = lax.rem(me, 2)
+    chip = me // 2
+    level = chip // 2
+    flank = lax.rem(chip, 2)
+    place = level + flank * (chips - 1 - 2 * level)
+
+    def device_at(position, kernel):
+        turned = position // side_chips
+        return 2 * (2 * position + turned * (2 * chips - 1 - 4 * position)) + kernel
+
+    onward = (
+        device_at(lax.rem(place + 1, chips), core),
+        device_at(lax.rem(place + chips - 1, chips), core),
+    )
+    partner = me + 1 - 2 * core
+
+    def origin(direction, hop):
+        shift = chips - hop if direction == 0 else hop
+        return lax.rem(place + shift, chips)
+
+    def lines_of(device):
+        return pl.ds(pl.multiple_of(device * lines, lines), lines)
+
+    def ring(k, direction, half, hop, distance):
+        ref = held.at[
+            k,
+            lines_of(device_at(origin(direction, distance), core)),
+            pl.ds(half * half_lanes, half_lanes),
+        ]
+        return pltpu.make_async_remote_copy(
+            src_ref=ref,
+            dst_ref=ref,
+            send_sem=ring_send.at[k, direction, half, hop - 1],
+            recv_sem=ring_recv.at[k, direction, half, hop - 1],
+            device_id={"row": onward[direction]},
+            device_id_type=MESH,
+        )
+
+    def ring_start(k, direction, half, hop):
+        ring(k, direction, half, hop, hop - 1).start()
+
+    def ring_wait(k, direction, half, hop):
+        ring(k, direction, half, hop, hop).wait_recv()
+
+    def share(k, slot, kernel):
+        direction = 0 if slot <= far else 1
+        hop = slot if slot <= far else slot - far
+        ref = held.at[k, lines_of(device_at(origin(direction, hop), kernel))]
+        return pltpu.make_async_remote_copy(
+            src_ref=ref,
+            dst_ref=ref,
+            send_sem=share_send.at[k, slot],
+            recv_sem=share_recv.at[k, slot],
+            device_id={"row": partner},
+            device_id_type=MESH,
+        )
+
+    def begin(k):
+        for half in range(2):
+            for direction in range(2):
+                ring_start(k, direction, half, 1)
+        share(k, 0, core).start()
+
+    def left_copy(step, target, source):
+        return pltpu.make_async_remote_copy(
+            src_ref=left_in.at[:, pl.ds(pl.multiple_of(target * left_lanes, left_lanes), left_lanes)],
+            dst_ref=left_held.at[lines_of(source)],
+            send_sem=left_send.at[step - 1],
+            recv_sem=left_recv.at[step - 1],
+            device_id={"row": target},
+            device_id_type=MESH,
+        )
+
+    def outer_steps(k, first, last):
+        @pl.loop(first, last)
+        def _(step):
+            part = jnp.dot(
+                left_t[...],
+                held[k, :, pl.ds(pl.multiple_of(step * (2 * span), 2 * span), 2 * span)],
+                preferred_element_type=jnp.float32,
+            )
+            part = part.astype(jnp.bfloat16).reshape(rows // 2, 2, width, 2 * span)
+            for half in range(2):
+                spot = pl.ds(pl.multiple_of(step * (2 * width) + half * width, width), width)
+                for side in range(2):
+                    outer[:, spot, side * span : (side + 1) * span] = part[
+                        :, side, :, half * span : (half + 1) * span
+                    ]
+
+    def map_steps(k, first, last):
+        @pl.loop(first, last)
+        def _(pair):
+            mapped = jnp.dot(map_t[...], outer[pair], preferred_element_type=jnp.float32)
+            mapped = mapped * (1.0 / count) + map_bias[...]
+            for side in range(2):
+                block = 2 * pair + side
+                row = lax.rem(block, fold) * SUBLANES + block // fold
+                out[row, pl.ds(pl.multiple_of(k * span, span), span), :] = mapped[
+                    :, side * span : (side + 1) * span
+                ].T.astype(jnp.bfloat16)
+
+    barrier = pltpu.get_barrier_semaphore()
+
+    @pl.loop(1, ways)
     def _(step):
-        part = jnp.dot(
-            left_t[...],
-            right[:, pl.ds(pl.multiple_of(step * (2 * span), 2 * span), 2 * span)],
-            preferred_element_type=jnp.float32,
-        )
-        part = part.astype(jnp.bfloat16).reshape(rows // 2, 2, width, 2 * span)
-        for half in range(2):
-            place = pl.ds(pl.multiple_of(step * (2 * width) + half * width, width), width)
-            for side in range(2):
-                outer[:, place, side * span : (side + 1) * span] = part[
-                    :, side, :, half * span : (half + 1) * span
-                ]
-
-    @pl.loop(0, rows // 2)
-    def _(pair):
-        mapped = jnp.dot(map_t[...], outer[pair], preferred_element_type=jnp.float32)
-        mapped = mapped * (1.0 / count) + map_bias[...]
-        for side in range(2):
-            block = 2 * pair + side
-            row = (block % fold) * SUBLANES + block // fold
-            out[row] = mapped[:, side * span : (side + 1) * span].T.astype(jnp.bfloat16)
-
-
-def pair_update(left_t, right, final_map_kernel, final_map_bias, rows):
-    count = right.shape[0]
+        pl.semaphore_signal(
+            barrier, inc=1, device_id={"row": lax.rem(me + step, ways)}, device_id_type=MESH
+        )
+
+    for k in range(chunks):
+        held[k, lines_of(me), :] = right_in[:, k * chunk_lanes : (k + 1) * chunk_lanes]
+    pl.semaphore_wait(barrier, ways - 1)
+
+    @pl.loop(1, ways)
+    def _(step):
+        left_copy(step, lax.rem(me + step, ways), me).start()
+
+    begin(0)
+    left_held[lines_of(me), :] = left_in[
+        :, pl.ds(pl.multiple_of(me * left_lanes, left_lanes), left_lanes)
+    ]
+
+    quarter = width // 8
+    third = rows // 2 // 4
+
+    @pl.loop(0, chunks)
+    def _(k):
+        def beside(work, number, size):
+            @pl.when(k > 0)
+            def _():
+                work(k - 1, number * size, (number + 1) * size)
+
+        for hop in range(1, far):
+            for half in range(2):
+                for direction in range(2):
+                    ring_wait(k, direction, half, hop)
+                    if hop + 1 < far or half == direction:
+                        ring_start(k, direction, half, hop + 1)
+                if half == 1:
+                    share(k, hop, core).start()
+                    share(k, far + hop, core).start()
+                    if hop == 1:
+
+                        @pl.when(k + 1 < chunks)
+                        def _():
+                            begin(k + 1)
+
+                number = 2 * (hop - 1) + half
+                if number < 4:
+                    beside(outer_steps, number, quarter)
+                else:
+                    beside(map_steps, number - 4, third)
+        ring_wait(k, 0, 0, far)
+        ring_wait(k, 1, 1, far)
+        share(k, far, core).start()
+        beside(map_steps, 2, third)
+        beside(map_steps, 3, third)
+
+        for slot in range(chips):
+            share(k, slot, 1 - core).wait_recv()
+
+        @pl.when(k == 0)
+        def _():
+            @pl.loop(1, ways)
+            def _(step):
+                source = lax.rem(me + ways - step, ways)
+                left_copy(step, lax.rem(me + step, ways), source).wait_recv()
+
+            for at in range(0, left_lanes, 2 * LANES):
+                left_t[at : at + 2 * LANES, :] = (
+                    left_held[:, at : at + 2 * LANES].astype(jnp.float32).T.astype(jnp.bfloat16)
+                )
+
+    outer_steps(chunks - 1, 0, width // 2)
+    map_steps(chunks - 1, 0, rows // 2)
+
+    @pl.loop(1, ways)
+    def _(step):
+        left_copy(step, lax.rem(me + step, ways), me).wait_send()
+
+    @pl.loop(0, chunks)
+    def _(k):
+        for direction in range(2):
+            for half in range(2):
+                for hop in range(1, far + 1):
+                    if hop < far or half == direction:
+                        ring(k, direction, half, hop, hop - 1).wait_send()
+        for slot in range(chips):
+            share(k, slot, core).wait_send()
+
+
+def exchange_and_pair(left, right, final_map_kernel, final_map_bias, rows, ways):
+    lines = right.shape[0]
+    count = lines * ways
     pair_width = final_map_kernel.shape[1]
-    width = left_t.shape[0] // rows
-    cols = right.shape[1] // width
+    cols = rows * ways
+    width = right.shape[1] // cols
+    chunks = cols // LANES
+    chips = ways // 2
     map_t = final_map_kernel.reshape(width, width, pair_width).transpose(2, 1, 0)
     whole = pl.BlockSpec(memory_space=pltpu.VMEM)
     return pl.pallas_call(
-        pair_kernel,
-        grid=(cols // LANES,),
-        in_specs=[
-            whole,
-            pl.BlockSpec((count, LANES * width), lambda k: (0, k)),
-            whole,
-            whole,
+        functools.partial(fused_kernel, ways),
+        in_specs=[whole] * 4,
+        out_specs=whole,
+        out_shape=jax.ShapeDtypeStruct((rows, cols, pair_width), jnp.bfloat16),
+        scratch_shapes=[
+            pltpu.VMEM((chunks, count, LANES * width), jnp.bfloat16),
+            pltpu.VMEM((count, rows * width), jnp.bfloat16),
+            pltpu.VMEM((rows * width, count), jnp.bfloat16),
+            pltpu.VMEM((rows // 2, width * width, 2 * LANES), jnp.bfloat16),
+            pltpu.SemaphoreType.DMA((ways - 1,)),
+            pltpu.SemaphoreType.DMA((ways - 1,)),
+            pltpu.SemaphoreType.DMA((chunks, 2, 2, chips // 2)),
+            pltpu.SemaphoreType.DMA((chunks, 2, 2, chips // 2)),
+            pltpu.SemaphoreType.DMA((chunks, chips)),
+            pltpu.SemaphoreType.DMA((chunks, chips)),
         ],
-        out_specs=pl.BlockSpec((rows, LANES, pair_width), lambda k: (0, k, 0)),
-        out_shape=jax.ShapeDtypeStruct((rows, cols, pair_width), jnp.bfloat16),
-        scratch_shapes=[pltpu.VMEM((rows // 2, width * width, 2 * LANES), jnp.bfloat16)],
-        compiler_params=pltpu.CompilerParams(vmem_limit_bytes=48 * 1024 * 1024),
-    )(left_t, right, map_t.reshape(pair_width, width * width), final_map_bias.reshape(pair_width, 1))
+        compiler_params=pltpu.CompilerParams(
+            collective_id=0, has_side_effects=True, vmem_limit_bytes=48 * 1024 * 1024
+        ),
+    )(
+        left,
+        right,
+        map_t.reshape(pair_width, width * width),
+        final_map_bias.reshape(pair_width, 1),
+    )
 
 
 def body(
@@ -223,15 +432,9 @@
         second_factor_kernel,
         second_factor_shift,
     )
-    rows = alignment_features.shape[1] // lax.axis_size("row")
-    left_t = lax.all_to_all(left, "row", split_axis=1, concat_axis=0, tiled=True).T
-    return pair_update(
-        left_t,
-        lax.all_gather(right, "row", axis=0, tiled=True),
-        final_map_kernel,
-        final_map_shift,
-        rows,
-    )
+    ways = lax.axis_size("row")
+    rows = alignment_features.shape[1] // ways
+    return exchange_and_pair(left, right, final_map_kernel, final_map_shift, rows, ways)
 
 
 def plain_body(

time: 158 us -> 112 us (0.71)
  waiting for transfers between devices: 77.2 us -> 0 us
  Pallas kernels: 51.3 us -> 101 us
  between operations: 13.5 us -> 0.06 us
  starting transfers between devices: 7.39 us -> 0 us
  local copies, waits for them, and re-layouts: 7.38 us -> 9.91 us
    all_gather x1 -> x0, waiting for transfers between devices: 57 us -> none  [body(): lax.all_gather(right, 'row', axis=0, tiled=True)]
    pallas_call x1, Pallas kernels: 44.6 us -> 94.7 us  [exchange_and_pair(): pl.pallas_call(functools.partial(fused_kernel, ways), in_specs=[whole] *...]
    all_to_all x1 -> x0, waiting for transfers between devices: 20.2 us -> none  [body(): lax.all_to_all(left, 'row', split_axis=1, concat_axis=0, tiled=True)]
    all_to_all x1 -> x0, starting transfers between devices: 7.38 us -> none  [body(): lax.all_to_all(left, 'row', split_axis=1, concat_axis=0, tiled=True)]
    unnamed x13 -> x10, local copies, waits for them, and re-layouts: 4.3 us -> 6.3 us
  transfers between devices with their start and end apart: 2 -> 0, of which waited for: 2 -> 0; matrix products, arithmetic and copies ran while one was open for 1% -> 0% of each run, Pallas kernels for 0% -> 0%
where the time goes in v2:
time: 112 us
  Pallas kernels  101 us (90%)
  local copies, waits for them, and re-layouts  9.91 us (9%)
    pallas_call x1, Pallas kernels, exchange_and_pair(): pl.pallas_call(functools.partial(fused_kernel, ways), in_specs=[whole] *...  94.7 us
    unnamed x10, local copies, waits for them, and re-layouts  6.3 us
    pallas_call x1, Pallas kernels, project(): pl.pallas_call(project_kernel, grid=(chunks,), in_specs=[pl.BlockSpec((li...  6.17 us

profile of v2, /device:TPU:0, one launch (start us, length us, event | category | flops | bytes accessed | tf_op | source)
XLA Modules:
  0.0 111.7 jit_solution(4921524164147760073)
XLA Ops:
  0.0 0.7 tile.2
  0.7 0.1 reshape_tile.3.first_bias
  0.7 0.7 copy.19.second_bias
  1.5 0.8 copy.22.map_bias
  2.2 0.9 broadcast_multiply_fusion
  3.2 0.2 copy.18.first_spread
  3.3 1.1 copy.20
  4.4 0.1 copy.21.map_t
  4.6 0.0 copy-start
  4.6 2.2 %copy-done = bf16[16,512,256]{2,1,0:T(8,128)(2,1)S(1)} copy-done((bf16[16,512,256]{2,1,0:T(8,128)(2,1)S(1)}, bf16[16,512,256]{2,1,0:T(8,128)(2,1)}, u32[]{:S(2)}) %copy-start) | copy-done | bytes 4194328
  6.7 0.0 copy-start.1
  6.8 0.7 copy-done.1
  7.5 0.0 copy-start.2
  7.5 0.7 copy-done.2
  8.1 0.0 copy-start.3
  8.1 0.7 copy-done.3
  8.8 6.2 %shard_map.91 = (bf16[16,16384]{1,0:T(8,128)(2,1)S(1)}, bf16[16,16384]{1,0:T(8,128)(2,1)S(1)}) custom-call(bf16[16,512,256]{2,1,0:T(8,128)(2,1)S(1)} %copy-done, f32[1,256]{1,0:T(1,128)S(1)} %bitcast.16, f32[1,256]{1,0:T(1,128)S(1)} %bitcast.17, bf16[1024,128]{1,0:T(8,128)(2,1)S(1)} %copy.18.first_spread, f32[1,128]{1,0:T(1,128)S(1)} %reshape_tile.3.first_bias, ...), custom_call_target="tpu_custom_call" | custom-call | tf_op jit(solution)/shard_map/pallas_call | solution.py:127
  15.0 94.7 %shard_map.92 = bf16[32,512,128]{2,1,0:T(8,128)(2,1)S(1)} custom-call(bf16[16,16384]{1,0:T(8,128)(2,1)S(1)} %get-tuple-element.7.left_in, bf16[16,16384]{1,0:T(8,128)(2,1)S(1)} %get-tuple-element.8.right_in, bf16[128,1024]{1,0:T(8,128)(2,1)S(1)} %copy.21.map_t, f32[128,1]{1,0:T(8,128)S(1)} %copy.22.map_bias), custom_call_target="tpu_custom_call" | custom-call | tf_op jit(solution)/shard_map/pallas_call | solution.py:387
  109.7 2.0 %copy.25 = bf16[32,512,128]{2,1,0:T(8,128)(2,1)} copy(bf16[32,512,128]{2,1,0:T(8,128)(2,1)S(1)} %shard_map.92) | data formatting | bytes 8388608
  (2 shorter events, 0.0 us)
Async XLA Ops:
  4.6 2.2 %copy-start = (bf16[16,512,256]{2,1,0:T(8,128)(2,1)S(1)}, bf16[16,512,256]{2,1,0:T(8,128)(2,1)}, u32[]{:S(2)}) copy-start(bf16[16,512,256]{2,1,0:T(8,128)(2,1)} %features.1) | copy-start | bytes 12582916
  6.7 0.7 copy-start.1
  7.5 0.7 copy-start.2
  8.1 0.7 copy-start.3

commit v3 on v2

--- a/solution.py
+++ b/solution.py
@@ -69,12 +69,13 @@
     features,
     gain,
     offset,
-    first_spread,
+    first_t,
     first_bias,
     second_t,
     second_bias,
     left_out,
     right_out,
+    first_spread,
     first_rows,
     second_rows,
 ):
@@ -82,6 +83,13 @@
     width = second_t.shape[0]
     fold = LANES // width
     owners = span // (fold * SUBLANES)
+
+    @pl.when(pl.program_id(0) == 0)
+    def _():
+        first_spread[...] = jnp.zeros_like(first_spread)
+        for m in range(fold):
+            first_spread[m * width : (m + 1) * width, m * depth : (m + 1) * depth] = first_t[...]
+
     incoming = features[...].astype(jnp.float32).reshape(lines * span, depth)
     center = incoming - jnp.mean(incoming, axis=-1, keepdims=True)
     spread = jnp.mean(center * center, axis=-1, keepdims=True)
@@ -92,18 +100,18 @@
         axis=1,
     )
     first_rows[...] = (
-        jnp.dot(folded, first_spread[...], preferred_element_type=jnp.float32) + first_bias[...]
+        lax.dot_general(
+            folded, first_spread[...], (((1,), (1,)), ((), ())), preferred_element_type=jnp.float32
+        )
+        + jnp.concatenate([first_bias[...]] * fold, axis=1)
     )
     flat = normed.astype(jnp.bfloat16)
     for s in range(lines):
-        second_rows[s * width : (s + 1) * width, :] = (
-            lax.dot_general(
-                second_t[...],
-                flat[s * span : (s + 1) * span],
-                (((1,), (1,)), ((), ())),
-                preferred_element_type=jnp.float32,
-            )
-            + second_bias[...]
+        second_rows[s * width : (s + 1) * width, :] = lax.dot_general(
+            second_t[...],
+            flat[s * span : (s + 1) * span],
+            (((1,), (1,)), ((), ())),
+            preferred_element_type=jnp.float32,
         )
     per_line = owners * SUBLANES
     for q in range(per_line):
@@ -111,9 +119,9 @@
             pl.ds(q, lines, stride=per_line), :
         ].astype(jnp.bfloat16)
     for d in range(width):
-        right_out[:, d * span : (d + 1) * span] = second_rows[
-            pl.ds(d, lines, stride=width), :
-        ].astype(jnp.bfloat16)
+        right_out[:, d * span : (d + 1) * span] = (
+            second_rows[pl.ds(d, lines, stride=width), :] + second_bias[d]
+        ).astype(jnp.bfloat16)
 
 
 def project(features, gain, offset, first_kernel, first_bias, second_kernel, second_bias):
@@ -121,31 +129,32 @@
     width = first_kernel.shape[1]
     fold = LANES // width
     chunks = residues // LANES
-    first_spread = jnp.einsum("mn,ck->mcnk", jnp.eye(fold, dtype=first_kernel.dtype), first_kernel)
-    first_spread = first_spread.reshape(fold * depth, LANES)
     whole = pl.BlockSpec(memory_space=pltpu.VMEM)
     return pl.pallas_call(
         project_kernel,
         grid=(chunks,),
-        in_specs=[pl.BlockSpec((lines, LANES, depth), lambda k: (0, k, 0))] + [whole] * 6,
+        in_specs=[pl.BlockSpec((lines, LANES, depth), lambda k: (0, k, 0))]
+        + [whole] * 5
+        + [pl.BlockSpec(memory_space=pltpu.SMEM)],
         out_specs=[
             pl.BlockSpec((lines, LANES * width), lambda k: (0, k)),
             pl.BlockSpec((lines, LANES * width), lambda k: (0, k)),
         ],
         out_shape=[jax.ShapeDtypeStruct((lines, residues * width), jnp.bfloat16)] * 2,
         scratch_shapes=[
+            pltpu.VMEM((LANES, fold * depth), jnp.bfloat16),
             pltpu.VMEM((lines * LANES // fold, LANES), jnp.float32),
             pltpu.VMEM((lines * width, LANES), jnp.float32),
         ],
-        compiler_params=pltpu.CompilerParams(vmem_limit_bytes=48 * 1024 * 1024),
+        compiler_params=pltpu.CompilerParams(vmem_limit_bytes=58 * 1024 * 1024),
     )(
         features,
         gain.reshape(1, depth),
         offset.reshape(1, depth),
-        first_spread,
-        jnp.tile(first_bias, fold).reshape(1, LANES),
+        first_kernel.T,
+        first_bias.reshape(1, width),
         second_kernel.T,
-        second_bias.reshape(width, 1),
+        second_bias,
     )
 
 
@@ -156,13 +165,15 @@
     ways,
     left_in,
     right_in,
-    map_t,
+    map_in,
     map_bias,
     out,
     held,
     left_held,
     left_t,
     outer,
+    map_rows,
+    map_t,
     left_send,
     left_recv,
     ring_send,
@@ -276,13 +287,13 @@
         @pl.loop(first, last)
         def _(pair):
             mapped = jnp.dot(map_t[...], outer[pair], preferred_element_type=jnp.float32)
-            mapped = mapped * (1.0 / count) + map_bias[...]
+            mapped = mapped * (1.0 / count)
             for side in range(2):
                 block = 2 * pair + side
                 row = lax.rem(block, fold) * SUBLANES + block // fold
-                out[row, pl.ds(pl.multiple_of(k * span, span), span), :] = mapped[
-                    :, side * span : (side + 1) * span
-                ].T.astype(jnp.bfloat16)
+                out[row, pl.ds(pl.multiple_of(k * span, span), span), :] = (
+                    mapped[:, side * span : (side + 1) * span].T + map_bias[...]
+                ).astype(jnp.bfloat16)
 
     barrier = pltpu.get_barrier_semaphore()
 
@@ -308,43 +319,91 @@
     quarter = width // 8
     third = rows // 2 // 4
 
-    @pl.loop(0, chunks)
-    def _(k):
-        def beside(work, number, size):
-            @pl.when(k > 0)
+    map_rows[...] = map_in[...].astype(jnp.float32)
+    for at in range(0, width, fold):
+        block = [map_rows[pl.ds(at + d, width, stride=width), :] for d in range(fold)]
+        map_t[:, at * width : (at + fold) * width] = (
+            jnp.concatenate(block, axis=0).T.astype(jnp.bfloat16)
+        )
+
+    begin(1)
+    piece = width // 8
+
+    @pl.loop(0, chunks + 2)
+    def _(n):
+        young = n < chunks
+        old = jnp.logical_and(n >= 1, n <= chunks)
+        ready = n >= 2
+
+        def beside(*slices):
+            @pl.when(ready)
             def _():
-                work(k - 1, number * size, (number + 1) * size)
-
-        for hop in range(1, far):
-            for half in range(2):
+                for work, number in slices:
+                    work(n - 2, number * piece, (number + 1) * piece)
+
+        @pl.when(jnp.logical_and(n >= 1, n + 1 < chunks))
+        def _():
+            begin(n + 1)
+
+        for half in range(2):
+
+            @pl.when(old)
+            def _():
                 for direction in range(2):
-                    ring_wait(k, direction, half, hop)
-                    if hop + 1 < far or half == direction:
-                        ring_start(k, direction, half, hop + 1)
-                if half == 1:
-                    share(k, hop, core).start()
-                    share(k, far + hop, core).start()
-                    if hop == 1:
-
-                        @pl.when(k + 1 < chunks)
-                        def _():
-                            begin(k + 1)
-
-                number = 2 * (hop - 1) + half
-                if number < 4:
-                    beside(outer_steps, number, quarter)
-                else:
-                    beside(map_steps, number - 4, third)
-        ring_wait(k, 0, 0, far)
-        ring_wait(k, 1, 1, far)
-        share(k, far, core).start()
-        beside(map_steps, 2, third)
-        beside(map_steps, 3, third)
-
-        for slot in range(chips):
-            share(k, slot, 1 - core).wait_recv()
-
-        @pl.when(k == 0)
+                    ring_wait(n - 1, direction, half, far - 1)
+                    if half == direction:
+                        ring_start(n - 1, direction, half, far)
+
+            @pl.when(young)
+            def _():
+                for direction in range(2):
+                    ring_wait(n, direction, half, 1)
+                    ring_start(n, direction, half, 2)
+
+            beside((outer_steps, half))
+
+        @pl.when(old)
+        def _():
+            share(n - 1, far - 1, core).start()
+            share(n - 1, 2 * far - 1, core).start()
+
+        @pl.when(young)
+        def _():
+            share(n, 1, core).start()
+            share(n, far + 1, core).start()
+
+        beside((outer_steps, 2))
+        for half in range(2):
+
+            @pl.when(young)
+            def _():
+                for direction in range(2):
+                    ring_wait(n, direction, half, 2)
+                    ring_start(n, direction, half, 3)
+
+            beside((outer_steps, 3) if half == 0 else (map_steps, 0))
+
+        @pl.when(young)
+        def _():
+            share(n, 2, core).start()
+            share(n, far + 2, core).start()
+
+        @pl.when(old)
+        def _():
+            ring_wait(n - 1, 0, 0, far)
+            ring_wait(n - 1, 1, 1, far)
+            share(n - 1, far, core).start()
+
+        @pl.when(ready)
+        def _():
+            map_steps(n - 2, piece, rows // 2)
+
+        @pl.when(old)
+        def _():
+            for slot in range(chips):
+                share(n - 1, slot, 1 - core).wait_recv()
+
+        @pl.when(n == 1)
         def _():
             @pl.loop(1, ways)
             def _(step):
@@ -355,9 +414,6 @@
                 left_t[at : at + 2 * LANES, :] = (
                     left_held[:, at : at + 2 * LANES].astype(jnp.float32).T.astype(jnp.bfloat16)
                 )
-
-    outer_steps(chunks - 1, 0, width // 2)
-    map_steps(chunks - 1, 0, rows // 2)
 
     @pl.loop(1, ways)
     def _(step):
@@ -382,7 +438,6 @@
     width = right.shape[1] // cols
     chunks = cols // LANES
     chips = ways // 2
-    map_t = final_map_kernel.reshape(width, width, pair_width).transpose(2, 1, 0)
     whole = pl.BlockSpec(memory_space=pltpu.VMEM)
     return pl.pallas_call(
         functools.partial(fused_kernel, ways),
@@ -394,6 +449,8 @@
             pltpu.VMEM((count, rows * width), jnp.bfloat16),
             pltpu.VMEM((rows * width, count), jnp.bfloat16),
             pltpu.VMEM((rows // 2, width * width, 2 * LANES), jnp.bfloat16),
+            pltpu.VMEM((width * width, pair_width), jnp.float32),
+            pltpu.VMEM((pair_width, width * width), jnp.bfloat16),
             pltpu.SemaphoreType.DMA((ways - 1,)),
             pltpu.SemaphoreType.DMA((ways - 1,)),
             pltpu.SemaphoreType.DMA((chunks, 2, 2, chips // 2)),
@@ -407,8 +464,8 @@
     )(
         left,
         right,
-        map_t.reshape(pair_width, width * width),
-        final_map_bias.reshape(pair_width, 1),
+        final_map_kernel,
+        final_map_bias.reshape(1, pair_width),
     )
 
 

time: 112 us -> 101 us (0.902)
  local copies, waits for them, and re-layouts: 9.91 us -> 4.1 us
  Pallas kernels: 101 us -> 95.5 us
    pallas_call x1, Pallas kernels: 94.7 us -> 87.7 us  [exchange_and_pair(): pl.pallas_call(functools.partial(fused_kernel, ways), in_specs=[whole] *...]
    unnamed x10 -> x9, local copies, waits for them, and re-layouts: 6.3 us -> 4.1 us
    reshape x4 -> x0, local copies, waits for them, and re-layouts: 1.81 us -> none  [the longest x1 0.76 us: exchange_and_pair(): final_map_bias.reshape(pair_width, 1)]
    pallas_call x1, Pallas kernels: 6.17 us -> 7.8 us  [project(): pl.pallas_call(project_kernel, grid=(chunks,), in_specs=[pl.BlockSpec((li...]
where the time goes in v3:
time: 101 us; the launch traced here: 99.7 us
  Pallas kernels  95.5 us (95%)
  local copies, waits for them, and re-layouts  4.1 us (4%)
    pallas_call x1, Pallas kernels, exchange_and_pair(): pl.pallas_call(functools.partial(fused_kernel, ways), in_specs=[whole] *...  87.7 us
    pallas_call x1, Pallas kernels, project(): pl.pallas_call(project_kernel, grid=(chunks,), in_specs=[pl.BlockSpec((li...  7.8 us
    unnamed x9, local copies, waits for them, and re-layouts  4.1 us

profile of v3, /device:TPU:0, one launch (start us, length us, event | category | flops | bytes accessed | tf_op | source)
XLA Modules:
  0.0 99.7 jit_solution(17388346568407243435)
XLA Ops:
  0.0 0.0 copy-start.3
  0.0 0.0 copy-start.2
  0.0 7.8 %shard_map.91 = (bf16[16,16384]{1,0:T(8,128)(2,1)}, bf16[16,16384]{1,0:T(8,128)(2,1)}) custom-call(bf16[16,512,256]{2,1,0:T(8,128)(2,1)} %features.1, f32[1,256]{1,0:T(1,128)} %bitcast.9, f32[1,256]{1,0:T(1,128)} %bitcast.10, bf16[32,256]{1,0:T(8,128)(2,1)} %bitcast.7, f32[1,32]{1,0:T(1,128)} %bitcast.11, bf16[32,256]{1,0:T(8,128)(2,1)} %bitcast.8, ...), custom_call_target="tpu_custom_call" | custom-call | tf_op jit(solution)/shard_map/pallas_call | solution.py:133
  7.8 0.0 copy-done.3
  7.8 0.0 copy-done.2
  7.8 0.0 copy-start
  7.8 1.0 %copy-done = bf16[16,16384]{1,0:T(8,128)(2,1)S(1)} copy-done((bf16[16,16384]{1,0:T(8,128)(2,1)S(1)}, bf16[16,16384]{1,0:T(8,128)(2,1)}, u32[]{:S(2)}) %copy-start) | copy-done | bytes 524312
  8.9 0.0 copy-start.1
  8.9 1.0 %copy-done.1 = bf16[16,16384]{1,0:T(8,128)(2,1)S(1)} copy-done((bf16[16,16384]{1,0:T(8,128)(2,1)S(1)}, bf16[16,16384]{1,0:T(8,128)(2,1)}, u32[]{:S(2)}) %copy-start.1) | copy-done | bytes 524312
  9.9 87.7 %shard_map.92 = bf16[32,512,128]{2,1,0:T(8,128)(2,1)S(1)} custom-call(bf16[16,16384]{1,0:T(8,128)(2,1)S(1)} %copy-done, bf16[16,16384]{1,0:T(8,128)(2,1)S(1)} %copy-done.1, bf16[1024,128]{1,0:T(8,128)(2,1)S(1)} %copy-done.2, f32[1,128]{1,0:T(1,128)S(1)} %bitcast.6), custom_call_target="tpu_custom_call" | custom-call | tf_op jit(solution)/shard_map/pallas_call | solution.py:442
  97.7 2.0 %copy.11 = bf16[32,512,128]{2,1,0:T(8,128)(2,1)} copy(bf16[32,512,128]{2,1,0:T(8,128)(2,1)S(1)} %shard_map.92) | data formatting | bytes 8388608
Async XLA Ops:
  0.0 7.8 %copy-start.3 = (f32[128]{0:T(128)S(1)}, f32[128]{0:T(128)}, u32[]{:S(2)}) copy-start(f32[128]{0:T(128)} %param.17) | copy-start | bytes 1540
  0.0 7.8 %copy-start.2 = (bf16[1024,128]{1,0:T(8,128)(2,1)S(1)}, bf16[1024,128]{1,0:T(8,128)(2,1)}, u32[]{:S(2)}) copy-start(bf16[1024,128]{1,0:T(8,128)(2,1)} %map_in.1) | copy-start | bytes 786436
  7.8 1.0 %copy-start = (bf16[16,16384]{1,0:T(8,128)(2,1)S(1)}, bf16[16,16384]{1,0:T(8,128)(2,1)}, u32[]{:S(2)}) copy-start(bf16[16,16384]{1,0:T(8,128)(2,1)} %get-tuple-element.7.left_in) | copy-start | bytes 1572868
  8.9 1.0 %copy-start.1 = (bf16[16,16384]{1,0:T(8,128)(2,1)S(1)}, bf16[16,16384]{1,0:T(8,128)(2,1)}, u32[]{:S(2)}) copy-start(bf16[16,16384]{1,0:T(8,128)(2,1)} %get-tuple-element.8.right_in) | copy-start | bytes 1572868

commit v4 on v3

--- a/solution.py
+++ b/solution.py
@@ -270,21 +270,25 @@
     def outer_steps(k, first, last):
         @pl.loop(first, last)
         def _(step):
-            part = jnp.dot(
-                left_t[...],
-                held[k, :, pl.ds(pl.multiple_of(step * (2 * span), 2 * span), 2 * span)],
-                preferred_element_type=jnp.float32,
-            )
-            part = part.astype(jnp.bfloat16).reshape(rows // 2, 2, width, 2 * span)
-            for half in range(2):
-                spot = pl.ds(pl.multiple_of(step * (2 * width) + half * width, width), width)
-                for side in range(2):
-                    outer[:, spot, side * span : (side + 1) * span] = part[
-                        :, side, :, half * span : (half + 1) * span
-                    ]
+            block = rows // 8
+            for group in range(4):
+                part = jnp.dot(
+                    left_t[group * 2 * block * width : (group + 1) * 2 * block * width, :],
+                    held[k, :, pl.ds(pl.multiple_of(step * (2 * span), 2 * span), 2 * span)],
+                    preferred_element_type=jnp.float32,
+                )
+                part = part.astype(jnp.bfloat16).reshape(block, 2, width, 2 * span)
+                for half in range(2):
+                    spot = pl.ds(pl.multiple_of(step * (2 * width) + half * width, width), width)
+                    for side in range(2):
+                        outer[
+                            group * block : (group + 1) * block,
+                            spot,
+                            side * span : (side + 1) * span,
+                        ] = part[:, side, :, half * span : (half + 1) * span]
 
     def map_steps(k, first, last):
-        @pl.loop(first, last)
+        @pl.loop(first, last, unroll=4)
         def _(pair):
             mapped = jnp.dot(map_t[...], outer[pair], preferred_element_type=jnp.float32)
             mapped = mapped * (1.0 / count)

time: 101 us -> 90.2 us (0.89); the launches traced: 99.7 us -> 90 us
  Pallas kernels: 95.5 us -> 85.9 us
    pallas_call x1, Pallas kernels: 87.7 us -> 78.1 us  [exchange_and_pair(): pl.pallas_call(functools.partial(fused_kernel, ways), in_specs=[whole] *...]
where the time goes in v4:
time: 90.2 us; the launch traced here: 90 us
  Pallas kernels  85.9 us (95%)
  local copies, waits for them, and re-layouts  4.1 us (5%)
    pallas_call x1, Pallas kernels, exchange_and_pair(): pl.pallas_call(functools.partial(fused_kernel, ways), in_specs=[whole] *...  78.1 us
    pallas_call x1, Pallas kernels, project(): pl.pallas_call(project_kernel, grid=(chunks,), in_specs=[pl.BlockSpec((li...  7.8 us
    unnamed x9, local copies, waits for them, and re-layouts  4.1 us

profile of v4, /device:TPU:0, one launch (start us, length us, event | category | flops | bytes accessed | tf_op | source)
XLA Modules:
  0.0 90.0 jit_solution(8495736399784151894)
XLA Ops:
  0.0 0.0 copy-start.3
  0.0 0.0 copy-start.2
  0.0 7.8 %shard_map.91 = (bf16[16,16384]{1,0:T(8,128)(2,1)}, bf16[16,16384]{1,0:T(8,128)(2,1)}) custom-call(bf16[16,512,256]{2,1,0:T(8,128)(2,1)} %features.1, f32[1,256]{1,0:T(1,128)} %bitcast.9, f32[1,256]{1,0:T(1,128)} %bitcast.10, bf16[32,256]{1,0:T(8,128)(2,1)} %bitcast.7, f32[1,32]{1,0:T(1,128)} %bitcast.11, bf16[32,256]{1,0:T(8,128)(2,1)} %bitcast.8, ...), custom_call_target="tpu_custom_call" | custom-call | tf_op jit(solution)/shard_map/pallas_call | solution.py:133
  7.8 0.0 copy-done.3
  7.8 0.0 copy-done.2
  7.8 0.0 copy-start
  7.8 1.0 %copy-done = bf16[16,16384]{1,0:T(8,128)(2,1)S(1)} copy-done((bf16[16,16384]{1,0:T(8,128)(2,1)S(1)}, bf16[16,16384]{1,0:T(8,128)(2,1)}, u32[]{:S(2)}) %copy-start) | copy-done | bytes 524312
  8.9 0.0 copy-start.1
  8.9 1.0 %copy-done.1 = bf16[16,16384]{1,0:T(8,128)(2,1)S(1)} copy-done((bf16[16,16384]{1,0:T(8,128)(2,1)S(1)}, bf16[16,16384]{1,0:T(8,128)(2,1)}, u32[]{:S(2)}) %copy-start.1) | copy-done | bytes 524312
  9.9 78.1 %shard_map.92 = bf16[32,512,128]{2,1,0:T(8,128)(2,1)S(1)} custom-call(bf16[16,16384]{1,0:T(8,128)(2,1)S(1)} %copy-done, bf16[16,16384]{1,0:T(8,128)(2,1)S(1)} %copy-done.1, bf16[1024,128]{1,0:T(8,128)(2,1)S(1)} %copy-done.2, f32[1,128]{1,0:T(1,128)S(1)} %bitcast.6), custom_call_target="tpu_custom_call" | custom-call | tf_op jit(solution)/shard_map/pallas_call | solution.py:446
  88.0 2.0 %copy.11 = bf16[32,512,128]{2,1,0:T(8,128)(2,1)} copy(bf16[32,512,128]{2,1,0:T(8,128)(2,1)S(1)} %shard_map.92) | data formatting | bytes 8388608
Async XLA Ops:
  0.0 7.8 %copy-start.3 = (f32[128]{0:T(128)S(1)}, f32[128]{0:T(128)}, u32[]{:S(2)}) copy-start(f32[128]{0:T(128)} %param.17) | copy-start | bytes 1540
  0.0 7.8 %copy-start.2 = (bf16[1024,128]{1,0:T(8,128)(2,1)S(1)}, bf16[1024,128]{1,0:T(8,128)(2,1)}, u32[]{:S(2)}) copy-start(bf16[1024,128]{1,0:T(8,128)(2,1)} %map_in.1) | copy-start | bytes 786436
  7.8 1.0 %copy-start = (bf16[16,16384]{1,0:T(8,128)(2,1)S(1)}, bf16[16,16384]{1,0:T(8,128)(2,1)}, u32[]{:S(2)}) copy-start(bf16[16,16384]{1,0:T(8,128)(2,1)} %get-tuple-element.7.left_in) | copy-start | bytes 1572868
  8.9 1.0 %copy-start.1 = (bf16[16,16384]{1,0:T(8,128)(2,1)S(1)}, bf16[16,16384]{1,0:T(8,128)(2,1)}, u32[]{:S(2)}) copy-start(bf16[16,16384]{1,0:T(8,128)(2,1)} %get-tuple-element.8.right_in) | copy-start | bytes 1572868
